TPU v7x, 512 devices: a whole 4x8x8 slice. The times are simulated.
512 devices in a mesh: rep: 64 (over y, x, z_lo), ctx: 8 (over z_hi, core).
Axes of the slice: x: 4, y: 8, z: 8 (z_hi: 4, z_lo: 2; z = z_hi * 2 + z_lo), core: 2. Of those that a mesh axis runs over, the one named last changes fastest.
Arguments:
- hidden: bfloat16 [64, 1024, 3584], P('rep', 'ctx'), may hold values from -6 to 6
- queries: bfloat16 [64, 1024, 2048], P('rep', 'ctx'), may hold values from -16 to 16
- values: bfloat16 [64, 1024, 1024], P('rep', 'ctx'), may hold values from -6 to 6
- cotangent: bfloat16 [64, 1024, 2048], P('rep', 'ctx'), may hold values from -6 to 6
- key_weight: bfloat16 [64, 3584, 1024], P('rep', None, 'ctx'), may hold values from -0.09375 to 0.09375
- doc_ids: int32 [64, 1024], P('rep', 'ctx'), may hold values from 0 to 3, never falling along the last dimension, each value on 1 to 512 neighbouring positions
- round_index: int32 [3], replicated, may hold values from 0 to 5
Outputs:
- averaged: bfloat16 [64, 3584, 1024], P('rep', None, 'ctx')
- gradient: bfloat16 [64, 3584, 1024], P('rep', None, 'ctx')
Inputs may be any that keep to these rules, and one draw needn't show every extreme that they name: `doc_ids`: document numbers never fall along a replica's positions; each document holds at most 512 positions and one holds exactly that many. `round_index`: the same rounds for every replica.
All inputs are finite; a program needn't handle non-finite values.
Results may differ from a plain program's by a relative error of at most 0.019.
Values may be sent and summed in bfloat16 or wider, within the bound.
A program may use at most 64 MiB of HBM per device.

v0:
```python
from functools import partial

import jax
import jax.numpy as jnp
from jax import lax
from jax.experimental import pallas as pl
from jax.experimental.pallas import tpu as pltpu
from jax.sharding import PartitionSpec as P

MESH = pl.DeviceIdType.MESH

HDIM = 256
HEADS = 8
KVH = 4
GOSSIP = 3
N_CTX = 8
CHIPS = 4
ROWS = 128
CHUNKS = 4
RANKS = 6

softcap = 50.0
step_size = 0.0005


PIECES = 7
INNER = 3


def gossip_plan(bits):
    outer = tuple(bit for bit in bits if bit < INNER)
    inner = tuple(bit for bit in bits if bit >= INNER)
    if not (outer and inner):
        outer, inner = (), bits
    depth = 1 if outer else 0
    if len(inner) == 1:
        plan = [("swap", inner, depth)]
    else:
        plan = [("scatter", inner, depth), ("gather", inner, depth)]
    if outer:
        plan = [("scatter", outer, 0)] + plan + [("gather", outer, 0)]
    return plan


def gossip_kernel(bits, x, out, acc, landing, send_sem, recv_sem):
    me = lax.axis_index("rep")
    plan = gossip_plan(bits)
    stages = len(plan)
    reduced = max(s for s, (kind, _, _) in enumerate(plan) if kind != "gather")
    rows = x.shape[0] // PIECES
    digit = {bit: lax.rem(me // (1 << bit), 2) for bit in bits}

    def peers(group):
        place = sum(digit[bit] << i for i, bit in enumerate(group))
        others = []
        for flip in range(1, 1 << len(group)):
            device, there = me, 0
            for i, bit in enumerate(group):
                if flip >> i & 1:
                    device = device + (1 - 2 * digit[bit]) * (1 << bit)
                    there = there + ((1 - digit[bit]) << i)
                else:
                    there = there + (digit[bit] << i)
            others.append((device, there))
        return place, others

    groups = {group: peers(group) for _, group, _ in plan}
    met = [device for _, others in groups.values() for device, _ in others]
    barrier = pltpu.get_barrier_semaphore()
    for device in met:
        pl.semaphore_signal(barrier, inc=1, device_id={"rep": device}, device_id_type=MESH)
    pl.semaphore_wait(barrier, len(met))

    def region(piece, depth):
        base, size = piece * rows, rows
        if depth:
            group = plan[0][1]
            size //= 1 << len(group)
            base = base + groups[group][0] * size
        return base, size

    def at(ref, base, size):
        return ref.at[pl.ds(pl.multiple_of(base, 16), size), :]

    def landed(stage, slot, piece, size):
        return landing.at[stage, slot, pl.ds(pl.multiple_of(piece * size, 16), size), :]

    def transfers(piece, stage, arriving=False):
        kind, group, depth = plan[stage]
        base, size = region(piece, depth)
        src = x if stage == 0 else acc
        place, others = groups[group]
        part = size if kind == "swap" else size >> len(group)
        for slot, (device, there) in enumerate(others):
            if kind == "gather":
                sent = at(out, base + place * part, part)
                dst = at(out, base + there * part, part) if arriving else sent
            else:
                sent = at(src, base if kind == "swap" else base + there * part, part)
                dst = landed(stage, slot, piece, part)
            yield pltpu.make_async_remote_copy(
                src_ref=sent, dst_ref=dst, send_sem=send_sem.at[piece, stage, slot],
                recv_sem=recv_sem.at[piece, stage, slot], device_id={"rep": device},
                device_id_type=MESH,
            )

    def start(piece, stage):
        for copy in transfers(piece, stage):
            copy.start()

    def finish(piece, stage):
        for copy in transfers(piece, stage, arriving=True):
            copy.wait_recv()
        kind, group, depth = plan[stage]
        if kind != "gather":
            base, size = region(piece, depth)
            place, others = groups[group]
            if kind == "scatter":
                size >>= len(group)
                base = base + place * size
            total = at(x if stage == 0 else acc, base, size)[...].astype(jnp.float32)
            for slot in range(len(others)):
                total = total + landed(stage, slot, piece, size)[...].astype(jnp.float32)
            mean = total * (1.0 / (1 << len(group)))
            at(out if stage == reduced else acc, base, size)[...] = mean.astype(jnp.bfloat16)

    @pl.loop(0, PIECES)
    def _(piece):
        start(piece, 0)

    for stage in range(stages):

        @pl.loop(0, PIECES)
        def _(piece, stage=stage):
            finish(piece, stage)
            if stage + 1 < stages:
                start(piece, stage + 1)

    @pl.loop(0, PIECES)
    def _(piece):
        for stage in range(stages):
            for copy in transfers(piece, stage):
                copy.wait_send()


def gossip(bits, number):
    def run(stepped):
        shape = stepped.shape
        plan = gossip_plan(bits)
        sums = [s for s, (kind, _, _) in enumerate(plan) if kind != "gather"]
        slots = max((1 << len(group)) - 1 for _, group, _ in plan)
        deepest = max(shape[0] >> (0 if kind == "swap" else len(group)) for kind, group, _ in plan)
        vmem = pl.BlockSpec(memory_space=pltpu.VMEM)
        return pl.pallas_call(
            partial(gossip_kernel, bits),
            out_shape=jax.ShapeDtypeStruct(shape, jnp.bfloat16),
            in_specs=[vmem],
            out_specs=vmem,
            scratch_shapes=[
                pltpu.VMEM(shape, jnp.bfloat16),
                pltpu.VMEM((max(sums) + 1, slots, deepest, shape[1]), jnp.bfloat16),
            ]
            + [pltpu.SemaphoreType.DMA((PIECES, len(plan), slots))] * 2,
            compiler_params=pltpu.CompilerParams(
                collective_id=number, has_side_effects=True, vmem_limit_bytes=24 * 1024 * 1024
            ),
            name="gossip",
        )(stepped)

    return run


def gossip_rounds(stepped, mask):
    branches = []
    for case in range(1 << RANKS):
        bits = tuple(bit for bit in range(RANKS) if case >> bit & 1)
        if 1 <= len(bits) <= GOSSIP:
            branches.append(gossip(bits, 1 + case))
        else:
            branches.append(lambda kept: kept)
    return lax.switch(mask, branches, stepped)


def nt(a, b):
    return lax.dot_general(a, b, (((1,), (1,)), ((), ())), preferred_element_type=jnp.float32)


def gradient_kernel(
    hid, qry, val, cot, wgt, docs, rounds, grad, stepped, mask,
    hall, qall, call, vall, dall, wown, kbuf, dkacc, dksend, dkrecv, dkown,
    local, h_recv, h_send, q_recv, q_send, c_recv, c_send, v_recv, v_send, d_recv, d_send,
    k_recv, k_send, g_recv, g_send,
):
    me = lax.axis_index("ctx")
    chip = me // 2
    core = lax.rem(me, 2)
    sib = chip * 2 + (1 - core)
    up_chip = lax.rem(chip + 1, CHIPS)
    dn_chip = lax.rem(chip + 3, CHIPS)
    opp_chip = lax.rem(chip + 2, CHIPS)
    up = up_chip * 2 + core
    dn = dn_chip * 2 + core
    opp = opp_chip * 2 + core
    rows_of = ROWS // CHUNKS

    def send(src, dst, ssem, rsem, dev):
        return pltpu.make_async_remote_copy(
            src_ref=src, dst_ref=dst, send_sem=ssem, recv_sem=rsem,
            device_id={"ctx": dev}, device_id_type=MESH,
        )

    mask[0] = (1 << rounds[0]) | (1 << rounds[1]) | (1 << rounds[2])
    barrier = pltpu.get_barrier_semaphore()
    for other in (sib, up, dn):
        pl.semaphore_signal(barrier, inc=1, device_id={"ctx": other}, device_id_type=MESH)

    head = pl.ds(pl.multiple_of(me * HDIM, HDIM), HDIM)
    kv_head = pl.ds(pl.multiple_of(chip * HDIM, HDIM), HDIM)
    own_half = pl.ds(pl.multiple_of(core * 128, 128), 128)
    sib_half = pl.ds(pl.multiple_of((1 - core) * 128, 128), 128)
    local_copies = [
        pltpu.make_async_copy(hid, hall.at[me], local.at[0]),
        pltpu.make_async_copy(wgt, wown, local.at[1]),
        pltpu.make_async_copy(qry.at[:, head], qall.at[me], local.at[2]),
        pltpu.make_async_copy(cot.at[:, head], call.at[me], local.at[3]),
        pltpu.make_async_copy(val.at[:, kv_head], vall.at[me], local.at[4]),
    ]
    for copy in local_copies:
        copy.start()
    pl.semaphore_wait(barrier, 3)

    started = []

    def go(copy):
        copy.start()
        started.append(copy)

    def piece(k):
        return pl.ds(k * rows_of, rows_of)

    low = list(range(CHUNKS // 2))
    high = list(range(CHUNKS // 2, CHUNKS))

    def h_to(dev, origin, k, sem, src=None):
        slot = hall.at[origin, piece(k), :]
        go(send(slot if src is None else src, slot, h_send.at[sem], h_recv.at[origin, k], dev))

    def h_wait(origin, k):
        slot = hall.at[origin, piece(k), :]
        send(slot, slot, h_send.at[0], h_recv.at[origin, k], sib).wait_recv()

    for a, b in zip(low + high, high + low):
        h_to(up, me, a, a, hid.at[piece(a), :])
        h_to(dn, me, b, CHUNKS + b, hid.at[piece(b), :])
    for k in range(CHUNKS):
        h_to(sib, me, k, 2 * CHUNKS + k, hid.at[piece(k), :])
    sem = 3 * CHUNKS
    for a, b in zip(low, high):
        h_wait(dn, a)
        h_to(up, dn, a, sem, None)
        h_to(sib, dn, a, sem + 1, None)
        h_wait(up, b)
        h_to(dn, up, b, sem + 2, None)
        h_to(sib, up, b, sem + 3, None)
        sem += 4
    for k in low:
        h_wait(dn_chip * 2 + 1 - core, k)

    for other in range(1, N_CTX):
        dev = lax.rem(me + other, N_CTX)
        go(send(docs, dall.at[me], d_send.at[other], d_recv.at[me], dev))
    dall[me] = docs[...]

    for i, (far_chip, far) in enumerate(((up_chip, up), (dn_chip, dn), (opp_chip, opp))):
        for j in range(2):
            dev = far_chip * 2 + j
            feats = pl.ds(pl.multiple_of(dev * HDIM, HDIM), HDIM)
            go(send(qry.at[:, feats], qall.at[me], q_send.at[2 * i + j], q_recv.at[me], dev))
            go(send(cot.at[:, feats], call.at[me], c_send.at[2 * i + j], c_recv.at[me], dev))
        feats = pl.ds(pl.multiple_of(far_chip * HDIM, HDIM), HDIM)
        go(send(val.at[:, feats], vall.at[me], v_send.at[i], v_recv.at[me], far))
    sib_feats = pl.ds(pl.multiple_of(sib * HDIM, HDIM), HDIM)
    go(send(qry.at[:, sib_feats], qall.at[me], q_send.at[6], q_recv.at[me], sib))
    go(send(cot.at[:, sib_feats], call.at[me], c_send.at[6], c_recv.at[me], sib))
    go(send(val.at[:, kv_head], vall.at[me], v_send.at[3], v_recv.at[me], sib))

    for copy in local_copies:
        copy.wait()

    def project(p):
        block = hall[pl.ds(2 * p, 2)].reshape(2 * ROWS, hall.shape[2])
        out = jnp.dot(block, wown[...], preferred_element_type=jnp.float32)
        rows = pl.ds(pl.multiple_of(p * 2 * ROWS, 2 * ROWS), 2 * ROWS)
        kbuf[rows, own_half] = out.astype(jnp.bfloat16)
        go(send(kbuf.at[rows, own_half], kbuf.at[rows, own_half], k_send.at[p], k_recv.at[p], sib))

    for k in range(CHUNKS):
        h_wait(sib, k)
    project(chip)

    for a, b in zip(high, low):
        h_wait(dn, a)
        h_to(sib, dn, a, sem, None)
        h_wait(up, b)
        h_to(sib, up, b, sem + 1, None)
        sem += 2
    for k in range(CHUNKS):
        h_wait(up_chip * 2 + 1 - core, k)
    project(up_chip)
    for k in high:
        h_wait(dn_chip * 2 + 1 - core, k)
    project(dn_chip)
    for a, b in zip(low, high):
        h_wait(opp, a)
        h_to(sib, opp, a, sem, None)
        h_wait(opp, b)
        h_to(sib, opp, b, sem + 1, None)
        sem += 2
    for k in range(CHUNKS):
        h_wait(opp_chip * 2 + 1 - core, k)
    project(opp_chip)

    for i, far in enumerate((up, dn, opp)):
        send(vall.at[far], vall.at[far], v_send.at[0], v_recv.at[far], sib).wait_recv()
        go(send(vall.at[far], vall.at[far], v_send.at[4 + i], v_recv.at[far], sib))
    for other in range(1, N_CTX):
        src = lax.rem(me + other, N_CTX)
        send(qall.at[src], qall.at[src], q_send.at[0], q_recv.at[src], sib).wait_recv()
        send(call.at[src], call.at[src], c_send.at[0], c_recv.at[src], sib).wait_recv()
        send(docs, dall.at[src], d_send.at[0], d_recv.at[src], sib).wait_recv()
    for p in (chip, up_chip, dn_chip, opp_chip):
        src = 2 * p + 1 - core
        send(vall.at[src], vall.at[src], v_send.at[0], v_recv.at[src], sib).wait_recv()
        rows = pl.ds(pl.multiple_of(p * 2 * ROWS, 2 * ROWS), 2 * ROWS)
        half = kbuf.at[rows, sib_half]
        send(half, half, k_send.at[0], k_recv.at[p], sib).wait_recv()

    doc_rows = [dall[s] for s in range(N_CTX)]
    starts = [jnp.zeros(row.shape, jnp.float32) for row in doc_rows]
    for v in range(3):
        total = jnp.zeros((1, 1), jnp.float32)
        for row in doc_rows:
            total = total + jnp.sum(jnp.where(row == v, 1.0, 0.0), axis=1, keepdims=True)
        starts = [s + jnp.where(row > v, total, 0.0) for s, row in zip(starts, doc_rows)]

    dkacc[...] = jnp.zeros_like(dkacc)
    block = 2 * ROWS
    for p in range(CHIPS):
        first = max(p - 2, 0)
        keys = (p + 1 - first) * block
        rows = pl.ds(first * block, keys)
        q = qall[2 * p : 2 * p + 2].reshape(block, HDIM)
        c = call[2 * p : 2 * p + 2].reshape(block, HDIM)
        v = vall[2 * first : 2 * p + 2].reshape(keys, HDIM)
        start = jnp.concatenate([starts[2 * p], starts[2 * p + 1]], axis=1).astype(jnp.int32)
        t = jnp.tanh(nt(kbuf[rows, :], q) * (1.0 / (HDIM**0.5 * softcap)))
        key_pos = first * block + lax.broadcasted_iota(jnp.int32, (keys, block), 0)
        query_pos = p * block + lax.broadcasted_iota(jnp.int32, (keys, block), 1)
        allowed = (key_pos <= query_pos) & (key_pos >= start)
        e = jnp.where(allowed, jnp.exp(softcap * t), 0.0)
        prob_grad = nt(v, c)
        norm = 1.0 / jnp.sum(e, axis=0, keepdims=True)
        row_dot = jnp.sum(e * prob_grad, axis=0, keepdims=True) * norm
        score_grad = (e * norm) * (prob_grad - row_dot) * (1.0 - t * t)
        dkacc[rows, :] += jnp.dot(
            score_grad.astype(jnp.bfloat16), q, preferred_element_type=jnp.float32
        )

    scale = 1.0 / HDIM**0.5
    dksend[...] = (dkacc[:, sib_half] * scale).astype(jnp.bfloat16)
    swap = send(dksend, dkrecv, g_send.at[0], g_recv.at[0], sib)
    go(swap)
    swap.wait_recv()
    dk = dkacc[:, own_half] * scale + dkrecv[...].astype(jnp.float32)
    dkown[...] = dk.T.astype(jnp.bfloat16)

    width = 512

    @pl.loop(0, grad.shape[0] // width)
    def _(i):
        cols = pl.ds(pl.multiple_of(i * width, width), width)
        h = hall[:, :, cols].reshape(N_CTX * ROWS, width)
        g = jnp.dot(dkown[...], h, preferred_element_type=jnp.float32).T
        grad[cols, :] = g.astype(jnp.bfloat16)
        stepped[cols, :] = (wown[cols, :].astype(jnp.float32) - step_size * g).astype(jnp.bfloat16)

    for copy in started:
        copy.wait_send()


def local_gradient(hidden, queries, values, cotangent, key_weight, doc_ids, round_index):
    depth = hidden.shape[1]
    dma = pltpu.SemaphoreType.DMA
    bf16, f32 = jnp.bfloat16, jnp.float32
    hbm = pl.BlockSpec(memory_space=pltpu.HBM)
    smem = pl.BlockSpec(memory_space=pltpu.SMEM)
    vmem = pl.BlockSpec(memory_space=pltpu.VMEM)
    seq = N_CTX * ROWS
    return pl.pallas_call(
        gradient_kernel,
        out_shape=[jax.ShapeDtypeStruct((depth, 128), bf16)] * 2
        + [jax.ShapeDtypeStruct((1,), jnp.int32)],
        in_specs=[hbm] * 5 + [vmem, smem],
        out_specs=[vmem, vmem, smem],
        scratch_shapes=[
            pltpu.VMEM((N_CTX, ROWS, depth), bf16),
            pltpu.VMEM((N_CTX, ROWS, HDIM), bf16),
            pltpu.VMEM((N_CTX, ROWS, HDIM), bf16),
            pltpu.VMEM((N_CTX, ROWS, HDIM), bf16),
            pltpu.VMEM((N_CTX, 1, ROWS), jnp.int32),
            pltpu.VMEM((depth, 128), bf16),
            pltpu.VMEM((seq, HDIM), bf16),
            pltpu.VMEM((seq, HDIM), f32),
            pltpu.VMEM((seq, 128), bf16),
            pltpu.VMEM((seq, 128), bf16),
            pltpu.VMEM((128, seq), bf16),
            dma((5,)),
            dma((N_CTX, CHUNKS)),
            dma((7 * CHUNKS,)),
            dma((N_CTX,)),
            dma((7,)),
            dma((N_CTX,)),
            dma((7,)),
            dma((N_CTX,)),
            dma((7,)),
            dma((N_CTX,)),
            dma((N_CTX,)),
            dma((CHIPS,)),
            dma((CHIPS,)),
            dma((1,)),
            dma((1,)),
        ],
        compiler_params=pltpu.CompilerParams(
            collective_id=0, has_side_effects=True, vmem_limit_bytes=60 * 1024 * 1024
        ),
        name="gradient",
    )(hidden, queries, values, cotangent, key_weight, doc_ids, round_index)


def on_device(hidden, queries, values, cotangent, key_weight, doc_ids, round_index):
    gradient, stepped, mask = local_gradient(
        hidden[0], queries[0], values[0], cotangent[0], key_weight[0], doc_ids, round_index
    )
    averaged = gossip_rounds(stepped, mask[0])
    return (averaged[None], gradient[None])


def solution(mesh):
    return jax.shard_map(
        on_device,
        mesh=mesh,
        in_specs=(
            P("rep", "ctx", None),
            P("rep", "ctx", None),
            P("rep", "ctx", None),
            P("rep", "ctx", None),
            P("rep", None, "ctx"),
            P("rep", "ctx"),
            P(),
        ),
        out_specs=(P("rep", None, "ctx"), P("rep", None, "ctx")),
        check_vma=False,
    )
```

profile of v0, /device:TPU:64, one launch (start us, length us, event | category | flops | bytes accessed | tf_op | source)
XLA Modules:
  0.0 146.2 jit_solution(10121144417836422092)
XLA Ops:
  0.6 111.6 %gradient.1 = (bf16[3584,128]{1,0:T(8,128)(2,1)}, bf16[3584,128]{1,0:T(8,128)(2,1)S(1)}, s32[1]{0:T(128)}) custom-call(bf16[128,3584]{1,0:T(8,128)(2,1)} %bitcast.10, bf16[128,2048]{1,0:T(8,128)(2,1)} %bitcast.12, bf16[128,1024]{1,0:T(8,128)(2,1)} %bitcast.14, bf16[128,2048]{1,0:T(8,128)(2,1)} %bitcast.13, bf16[3584,128]{1,0:T(8,128)(2,1)} %bitcast.11, ...), custom_call_target="tpu_custom_call" | custom-call | tf_op jit(solution)/shard_map/gradient/pallas_call | solution.py:399
  112.8 30.9 %conditional.1 = (bf16[3584,128]{1,0:T(8,128)(2,1)S(1)}) conditional(s32[]{:T(128)} %bitcast.5, bf16[3584,128]{1,0:T(8,128)(2,1)S(1)} %get-tuple-element.185, bf16[3584,128]{1,0:T(8,128)(2,1)S(1)} %get-tuple-element.185, bf16[3584,128]{1,0:T(8,128)(2,1)S(1)} %get-tuple-element.185, ...), branch_computations={%region_0.0_spmd, %region_1.0_spmd, %region_2.0_spmd, %region_3.0_... | conditional | bytes 1835016 | solution.py:181
  113.1 30.7 %gossip.72 = bf16[3584,128]{1,0:T(8,128)(2,1)S(1)} custom-call(bf16[3584,128]{1,0:T(8,128)(2,1)S(1)} %x.31), custom_call_target="tpu_custom_call" | custom-call | tf_op jit(solution)/shard_map/cond/branch_38_fun/gossip/pallas_call | solution.py:154
  143.8 0.0 copy-start
  143.8 0.9 copy.75
  144.7 0.6 copy-done
  145.3 0.9 copy.76
Async XLA Ops:
  143.8 1.5 %copy-start = (bf16[3584,128]{1,0:T(8,128)(2,1)S(1)}, bf16[3584,128]{1,0:T(8,128)(2,1)}, u32[]{:S(2)}) copy-start(bf16[3584,128]{1,0:T(8,128)(2,1)} %get-tuple-element.186) | copy-start | bytes 2752516
where the time goes:
time: 146 us
  Pallas kernels  142 us (97%)
  local copies, waits for them, and re-layouts  2.42 us (2%)
    pallas_call x1, Pallas kernels, local_gradient(): pl.pallas_call(gradient_kernel, out_shape=[jax.ShapeDtypeStruct((depth, 1...  112 us
    pallas_call x1, Pallas kernels, run(): pl.pallas_call(partial(gossip_kernel, bits), out_shape=jax.ShapeDtypeStru...  30.7 us

commit v1 on v0

--- a/solution.py
+++ b/solution.py
@@ -1,3 +1,4 @@
+import itertools
 from functools import partial
 
 import jax
@@ -17,6 +18,7 @@
 CHIPS = 4
 ROWS = 128
 CHUNKS = 4
+AHEAD = 2
 RANKS = 6
 
 softcap = 50.0
@@ -187,7 +189,7 @@
 
 def gradient_kernel(
     hid, qry, val, cot, wgt, docs, rounds, grad, stepped, mask,
-    hall, qall, call, vall, dall, wown, kbuf, dkacc, dksend, dkrecv, dkown,
+    hall, qall, call, vall, dall, wown, kbuf, dkacc, dksend, dkrecv, dkown, first_pos,
     local, h_recv, h_send, q_recv, q_send, c_recv, c_send, v_recv, v_send, d_recv, d_send,
     k_recv, k_send, g_recv, g_send,
 ):
@@ -195,8 +197,9 @@
     chip = me // 2
     core = lax.rem(me, 2)
     sib = chip * 2 + (1 - core)
-    up_chip = lax.rem(chip + 1, CHIPS)
-    dn_chip = lax.rem(chip + 3, CHIPS)
+    way = 1 - 2 * lax.rem(lax.axis_index("rep"), 2)
+    up_chip = lax.rem(chip + CHIPS + way, CHIPS)
+    dn_chip = lax.rem(chip + CHIPS - way, CHIPS)
     opp_chip = lax.rem(chip + 2, CHIPS)
     up = up_chip * 2 + core
     dn = dn_chip * 2 + core
@@ -238,8 +241,8 @@
     def piece(k):
         return pl.ds(k * rows_of, rows_of)
 
-    low = list(range(CHUNKS // 2))
-    high = list(range(CHUNKS // 2, CHUNKS))
+    low = list(range(AHEAD))
+    high = list(range(AHEAD, CHUNKS))
 
     def h_to(dev, origin, k, sem, src=None):
         slot = hall.at[origin, piece(k), :]
@@ -254,35 +257,42 @@
         h_to(dn, me, b, CHUNKS + b, hid.at[piece(b), :])
     for k in range(CHUNKS):
         h_to(sib, me, k, 2 * CHUNKS + k, hid.at[piece(k), :])
-    sem = 3 * CHUNKS
-    for a, b in zip(low, high):
+    sem = itertools.count(3 * CHUNKS)
+
+    def pass_on(i):
+        a, b = (low + high)[i], (high + low)[i]
         h_wait(dn, a)
-        h_to(up, dn, a, sem, None)
-        h_to(sib, dn, a, sem + 1, None)
+        if a in low:
+            h_to(up, dn, a, next(sem))
+        h_to(sib, dn, a, next(sem))
         h_wait(up, b)
-        h_to(dn, up, b, sem + 2, None)
-        h_to(sib, up, b, sem + 3, None)
-        sem += 4
-    for k in low:
-        h_wait(dn_chip * 2 + 1 - core, k)
+        if b in high:
+            h_to(dn, up, b, next(sem))
+        h_to(sib, up, b, next(sem))
+
+    for i in range(CHUNKS // 2):
+        pass_on(i)
+    h_wait(dn_chip * 2 + 1 - core, low[0])
 
     for other in range(1, N_CTX):
         dev = lax.rem(me + other, N_CTX)
         go(send(docs, dall.at[me], d_send.at[other], d_recv.at[me], dev))
     dall[me] = docs[...]
 
-    for i, (far_chip, far) in enumerate(((up_chip, up), (dn_chip, dn), (opp_chip, opp))):
+    far_chips = ((opp_chip, opp), (up_chip, up), (dn_chip, dn))
+    for i, (far_chip, far) in enumerate(far_chips):
+        feats = pl.ds(pl.multiple_of(far_chip * HDIM, HDIM), HDIM)
+        go(send(val.at[:, feats], vall.at[me], v_send.at[i], v_recv.at[me], far))
+    go(send(val.at[:, kv_head], vall.at[me], v_send.at[3], v_recv.at[me], sib))
+    sib_feats = pl.ds(pl.multiple_of(sib * HDIM, HDIM), HDIM)
+    go(send(qry.at[:, sib_feats], qall.at[me], q_send.at[6], q_recv.at[me], sib))
+    go(send(cot.at[:, sib_feats], call.at[me], c_send.at[6], c_recv.at[me], sib))
+    for i, (far_chip, far) in enumerate(far_chips):
         for j in range(2):
             dev = far_chip * 2 + j
             feats = pl.ds(pl.multiple_of(dev * HDIM, HDIM), HDIM)
             go(send(qry.at[:, feats], qall.at[me], q_send.at[2 * i + j], q_recv.at[me], dev))
             go(send(cot.at[:, feats], call.at[me], c_send.at[2 * i + j], c_recv.at[me], dev))
-        feats = pl.ds(pl.multiple_of(far_chip * HDIM, HDIM), HDIM)
-        go(send(val.at[:, feats], vall.at[me], v_send.at[i], v_recv.at[me], far))
-    sib_feats = pl.ds(pl.multiple_of(sib * HDIM, HDIM), HDIM)
-    go(send(qry.at[:, sib_feats], qall.at[me], q_send.at[6], q_recv.at[me], sib))
-    go(send(cot.at[:, sib_feats], call.at[me], c_send.at[6], c_recv.at[me], sib))
-    go(send(val.at[:, kv_head], vall.at[me], v_send.at[3], v_recv.at[me], sib))
 
     for copy in local_copies:
         copy.wait()
@@ -298,24 +308,17 @@
         h_wait(sib, k)
     project(chip)
 
-    for a, b in zip(high, low):
-        h_wait(dn, a)
-        h_to(sib, dn, a, sem, None)
-        h_wait(up, b)
-        h_to(sib, up, b, sem + 1, None)
-        sem += 2
+    for i in range(CHUNKS // 2, CHUNKS):
+        pass_on(i)
     for k in range(CHUNKS):
         h_wait(up_chip * 2 + 1 - core, k)
     project(up_chip)
-    for k in high:
+    for k in range(1, CHUNKS):
         h_wait(dn_chip * 2 + 1 - core, k)
     project(dn_chip)
-    for a, b in zip(low, high):
-        h_wait(opp, a)
-        h_to(sib, opp, a, sem, None)
-        h_wait(opp, b)
-        h_to(sib, opp, b, sem + 1, None)
-        sem += 2
+    for k in low + high:
+        h_wait(opp, k)
+        h_to(sib, opp, k, next(sem))
     for k in range(CHUNKS):
         h_wait(opp_chip * 2 + 1 - core, k)
     project(opp_chip)
@@ -325,15 +328,7 @@
         go(send(vall.at[far], vall.at[far], v_send.at[4 + i], v_recv.at[far], sib))
     for other in range(1, N_CTX):
         src = lax.rem(me + other, N_CTX)
-        send(qall.at[src], qall.at[src], q_send.at[0], q_recv.at[src], sib).wait_recv()
-        send(call.at[src], call.at[src], c_send.at[0], c_recv.at[src], sib).wait_recv()
         send(docs, dall.at[src], d_send.at[0], d_recv.at[src], sib).wait_recv()
-    for p in (chip, up_chip, dn_chip, opp_chip):
-        src = 2 * p + 1 - core
-        send(vall.at[src], vall.at[src], v_send.at[0], v_recv.at[src], sib).wait_recv()
-        rows = pl.ds(pl.multiple_of(p * 2 * ROWS, 2 * ROWS), 2 * ROWS)
-        half = kbuf.at[rows, sib_half]
-        send(half, half, k_send.at[0], k_recv.at[p], sib).wait_recv()
 
     doc_rows = [dall[s] for s in range(N_CTX)]
     starts = [jnp.zeros(row.shape, jnp.float32) for row in doc_rows]
@@ -342,21 +337,41 @@
         for row in doc_rows:
             total = total + jnp.sum(jnp.where(row == v, 1.0, 0.0), axis=1, keepdims=True)
         starts = [s + jnp.where(row > v, total, 0.0) for s, row in zip(starts, doc_rows)]
-
+    for p in range(CHIPS):
+        both = jnp.concatenate([starts[2 * p], starts[2 * p + 1]], axis=1)
+        first_pos[p] = both.astype(jnp.int32)
     dkacc[...] = jnp.zeros_like(dkacc)
+
+    for p in (chip, up_chip, dn_chip, opp_chip):
+        src = 2 * p + 1 - core
+        send(vall.at[src], vall.at[src], v_send.at[0], v_recv.at[src], sib).wait_recv()
+        rows = pl.ds(pl.multiple_of(p * 2 * ROWS, 2 * ROWS), 2 * ROWS)
+        half = kbuf.at[rows, sib_half]
+        send(half, half, k_send.at[0], k_recv.at[p], sib).wait_recv()
+
     block = 2 * ROWS
-    for p in range(CHIPS):
-        first = max(p - 2, 0)
-        keys = (p + 1 - first) * block
-        rows = pl.ds(first * block, keys)
-        q = qall[2 * p : 2 * p + 2].reshape(block, HDIM)
-        c = call[2 * p : 2 * p + 2].reshape(block, HDIM)
-        v = vall[2 * first : 2 * p + 2].reshape(keys, HDIM)
-        start = jnp.concatenate([starts[2 * p], starts[2 * p + 1]], axis=1).astype(jnp.int32)
+    keys = 3 * block
+
+    @pl.loop(0, CHIPS)
+    def _(turn):
+        p = lax.rem(chip + turn + (turn // 2) * (5 - 2 * turn), CHIPS)
+        for j in range(2):
+            src = 2 * p + j
+
+            @pl.when(src != me)
+            def _():
+                send(qall.at[src], qall.at[src], q_send.at[0], q_recv.at[src], sib).wait_recv()
+                send(call.at[src], call.at[src], c_send.at[0], c_recv.at[src], sib).wait_recv()
+
+        first = p // 3
+        rows = pl.ds(pl.multiple_of(first * block, block), keys)
+        q = qall[pl.ds(2 * p, 2)].reshape(block, HDIM)
+        c = call[pl.ds(2 * p, 2)].reshape(block, HDIM)
+        v = vall[pl.ds(2 * first, 6)].reshape(keys, HDIM)
         t = jnp.tanh(nt(kbuf[rows, :], q) * (1.0 / (HDIM**0.5 * softcap)))
         key_pos = first * block + lax.broadcasted_iota(jnp.int32, (keys, block), 0)
         query_pos = p * block + lax.broadcasted_iota(jnp.int32, (keys, block), 1)
-        allowed = (key_pos <= query_pos) & (key_pos >= start)
+        allowed = (key_pos <= query_pos) & (key_pos >= first_pos[p])
         e = jnp.where(allowed, jnp.exp(softcap * t), 0.0)
         prob_grad = nt(v, c)
         norm = 1.0 / jnp.sum(e, axis=0, keepdims=True)
@@ -414,6 +429,7 @@
             pltpu.VMEM((seq, 128), bf16),
             pltpu.VMEM((seq, 128), bf16),
             pltpu.VMEM((128, seq), bf16),
+            pltpu.VMEM((CHIPS, 1, 2 * ROWS), jnp.int32),
             dma((5,)),
             dma((N_CTX, CHUNKS)),
             dma((7 * CHUNKS,)),

time: 146 us -> 165 us (1.13)
  Pallas kernels: 142 us -> 161 us
    pallas_call x1, Pallas kernels: 30.7 us -> 52.1 us  [run(): pl.pallas_call(partial(gossip_kernel, bits), out_shape=jax.ShapeDtypeStru...]
    pallas_call x1, Pallas kernels: 112 us -> 109 us  [local_gradient(): pl.pallas_call(gradient_kernel, out_shape=[jax.ShapeDtypeStruct((depth, 1...]
where the time goes in v1:
time: 165 us
  Pallas kernels  161 us (98%)
  local copies, waits for them, and re-layouts  2.42 us (1%)
    pallas_call x1, Pallas kernels, local_gradient(): pl.pallas_call(gradient_kernel, out_shape=[jax.ShapeDtypeStruct((depth, 1...  109 us
    pallas_call x1, Pallas kernels, run(): pl.pallas_call(partial(gossip_kernel, bits), out_shape=jax.ShapeDtypeStru...  52.1 us

profile of v1, /device:TPU:64, one launch (start us, length us, event | category | flops | bytes accessed | tf_op | source)
XLA Modules:
  0.0 164.6 jit_solution(18074157159489353404)
XLA Ops:
  0.6 108.6 %gradient.1 = (bf16[3584,128]{1,0:T(8,128)(2,1)}, bf16[3584,128]{1,0:T(8,128)(2,1)S(1)}, s32[1]{0:T(128)}) custom-call(bf16[128,3584]{1,0:T(8,128)(2,1)} %bitcast.10, bf16[128,2048]{1,0:T(8,128)(2,1)} %bitcast.12, bf16[128,1024]{1,0:T(8,128)(2,1)} %bitcast.14, bf16[128,2048]{1,0:T(8,128)(2,1)} %bitcast.13, bf16[3584,128]{1,0:T(8,128)(2,1)} %bitcast.11, ...), custom_call_target="tpu_custom_call" | custom-call | tf_op jit(solution)/shard_map/gradient/pallas_call | solution.py:414
  109.8 52.3 %conditional.1 = (bf16[3584,128]{1,0:T(8,128)(2,1)S(1)}) conditional(s32[]{:T(128)} %bitcast.5, bf16[3584,128]{1,0:T(8,128)(2,1)S(1)} %get-tuple-element.185, bf16[3584,128]{1,0:T(8,128)(2,1)S(1)} %get-tuple-element.185, bf16[3584,128]{1,0:T(8,128)(2,1)S(1)} %get-tuple-element.185, ...), branch_computations={%region_0.0_spmd, %region_1.0_spmd, %region_2.0_spmd, %region_3.0_... | conditional | bytes 1835016 | solution.py:183
  110.1 52.1 %gossip.80 = bf16[3584,128]{1,0:T(8,128)(2,1)S(1)} custom-call(bf16[3584,128]{1,0:T(8,128)(2,1)S(1)} %x.39), custom_call_target="tpu_custom_call" | custom-call | tf_op jit(solution)/shard_map/cond/branch_52_fun/gossip/pallas_call | solution.py:156
  162.2 0.0 copy-start
  162.2 0.9 copy.75
  163.1 0.6 copy-done
  163.7 0.9 copy.76
Async XLA Ops:
  162.2 1.5 copy-start

commit v2 on v1

--- a/solution.py
+++ b/solution.py
@@ -32,7 +32,9 @@
 def gossip_plan(bits):
     outer = tuple(bit for bit in bits if bit < INNER)
     inner = tuple(bit for bit in bits if bit >= INNER)
-    if not (outer and inner):
+    if bits == (INNER, INNER + 1):
+        outer, inner = bits[:1], bits[1:]
+    elif not (outer and inner):
         outer, inner = (), bits
     depth = 1 if outer else 0
     if len(inner) == 1:
@@ -389,7 +391,7 @@
     dk = dkacc[:, own_half] * scale + dkrecv[...].astype(jnp.float32)
     dkown[...] = dk.T.astype(jnp.bfloat16)
 
-    width = 512
+    width = 896
 
     @pl.loop(0, grad.shape[0] // width)
     def _(i):

time: 165 us -> 173 us (1.048)
  the two profiles are of different devices: /device:TPU:64 before, /device:TPU:8 now
where the time goes in v2:
time: 173 us
  Pallas kernels  169 us (98%)
  local copies, waits for them, and re-layouts  2.42 us (1%)
    pallas_call x1, Pallas kernels, run(): pl.pallas_call(partial(gossip_kernel, bits), out_shape=jax.ShapeDtypeStru...  86.9 us
    pallas_call x1, Pallas kernels, local_gradient(): pl.pallas_call(gradient_kernel, out_shape=[jax.ShapeDtypeStruct((depth, 1...  82.3 us

profile of v2, /device:TPU:8, one launch (start us, length us, event | category | flops | bytes accessed | tf_op | source)
XLA Modules:
  0.0 173.2 jit_solution(10692802947567849946)
XLA Ops:
  0.6 82.3 %gradient.1 = (bf16[3584,128]{1,0:T(8,128)(2,1)}, bf16[3584,128]{1,0:T(8,128)(2,1)S(1)}, s32[1]{0:T(128)}) custom-call(bf16[128,3584]{1,0:T(8,128)(2,1)} %bitcast.10, bf16[128,2048]{1,0:T(8,128)(2,1)} %bitcast.12, bf16[128,1024]{1,0:T(8,128)(2,1)} %bitcast.14, bf16[128,2048]{1,0:T(8,128)(2,1)} %bitcast.13, bf16[3584,128]{1,0:T(8,128)(2,1)} %bitcast.11, ...), custom_call_target="tpu_custom_call" | custom-call | tf_op jit(solution)/shard_map/gradient/pallas_call | solution.py:416
  83.5 87.2 %conditional.1 = (bf16[3584,128]{1,0:T(8,128)(2,1)S(1)}) conditional(s32[]{:T(128)} %bitcast.5, bf16[3584,128]{1,0:T(8,128)(2,1)S(1)} %get-tuple-element.185, bf16[3584,128]{1,0:T(8,128)(2,1)S(1)} %get-tuple-element.185, bf16[3584,128]{1,0:T(8,128)(2,1)S(1)} %get-tuple-element.185, ...), branch_computations={%region_0.0_spmd, %region_1.0_spmd, %region_2.0_spmd, %region_3.0_... | conditional | bytes 1835016 | solution.py:185
  83.8 86.9 %gossip.81 = bf16[3584,128]{1,0:T(8,128)(2,1)S(1)} custom-call(bf16[3584,128]{1,0:T(8,128)(2,1)S(1)} %x.40), custom_call_target="tpu_custom_call" | custom-call | tf_op jit(solution)/shard_map/cond/branch_56_fun/gossip/pallas_call | solution.py:158
  170.7 0.0 copy-start
  170.7 0.9 copy.75
  171.7 0.6 copy-done
  172.2 0.9 copy.76
Async XLA Ops:
  170.7 1.5 copy-start
